TPU v7x, 128 devices: a whole 4x4x4 slice. The times are simulated.
128 devices in a mesh: pp: 2 (over core), fsdp: 16 (over y, x), tp: 4 (over z).
Axes of the slice: x: 4, y: 4, z: 4, core: 2. Of those that a mesh axis runs over, the one named last changes fastest.
Arguments:
- inputs: bfloat16 [2, 512, 8192], P(None, 'tp', 'fsdp'), may hold values from -12 to 12
- head_grad: bfloat16 [2, 512, 8192], P(None, 'tp', 'fsdp'), may hold values from -0.3 to 0.3
- noise_mask: int32 [2, 512], P(None, 'tp'), may hold values 0 or 1
- lengths: int32 [2, 16, 2], replicated, may hold values from 1 to 24, 32 in all within a row
- rewards: int32 [2, 16, 2], replicated, may hold values from 0 to 3
- groups: int32 [2, 16, 2], replicated, may hold values from 0 to 31, as said below
- query_weight: bfloat16 [2, 8192, 4096], P('pp', 'fsdp', 'tp'), may hold values from -0.0625 to 0.0625
- key_weight: bfloat16 [2, 8192, 1024], P('pp', 'fsdp', 'tp'), may hold values from -0.0625 to 0.0625
- value_weight: bfloat16 [2, 8192, 1024], P('pp', 'fsdp', 'tp'), may hold values from -1 to 1
- out_weight: bfloat16 [2, 4096, 8192], P('pp', 'tp', 'fsdp'), may hold values from -1 to 1
Outputs:
- query_weight_grad: float32 [2, 8192, 4096], P('pp', 'fsdp', 'tp')
- key_weight_grad: float32 [2, 8192, 1024], P('pp', 'fsdp', 'tp')
- value_weight_grad: float32 [2, 8192, 1024], P('pp', 'fsdp', 'tp')
- out_weight_grad: float32 [2, 4096, 8192], P('pp', 'tp', 'fsdp')
Inputs may be any that keep to these rules, and one draw needn't show every extreme that they name: `groups`: every group value names exactly 2 completions.
All inputs are finite; a program needn't handle non-finite values. No bound on the sum of `noise_mask` on one device may be relied on, other than what follows from the above.
Results may differ from a plain program's by a relative error of at most 0.013.
Values may be sent and summed in bfloat16 or wider, within the bound.
A program may use at most 128 MiB of HBM per device.

v0:
```python
import jax
import jax.numpy as jnp
from jax import lax
from jax.sharding import PartitionSpec as P

MODEL_WIDTH = 8192
HEAD_WIDTH = 128
SLOT = 32
epsilon = 1e-06
masked_score = -1e30


def segments(lengths):
    ends = jnp.stack([jnp.sum(lengths[..., : c + 1], -1) for c in range(lengths.shape[-1])], -1)
    position = jnp.arange(SLOT, dtype=jnp.int32)
    return jnp.sum((ends[..., None, :] <= position[:, None]).astype(jnp.int32), -1)


def token_weights(lengths, rewards, groups):
    group_total = 2 * lengths.shape[1]
    reward_flat = rewards.reshape(-1).astype(jnp.float32)
    member = (
        groups.reshape(-1)[:, None] == jnp.arange(group_total, dtype=jnp.int32)[None, :]
    ).astype(jnp.float32)
    member_count = jnp.sum(member, 0)
    group_mean = jnp.sum(member * reward_flat[:, None], 0) / member_count
    centered = reward_flat - jnp.sum(member * group_mean[None, :], 1)
    variance = jnp.sum(member * (centered * centered)[:, None], 0) / member_count
    spread_own = jnp.sum(member * jnp.sqrt(variance)[None, :], 1)
    advantage = (centered / jnp.maximum(spread_own, 1.0)).reshape(lengths.shape)
    segment = segments(lengths)
    choose = (segment[..., None] == jnp.arange(lengths.shape[2], dtype=jnp.int32)).astype(
        jnp.float32
    )
    token_adv = jnp.sum(choose * advantage[:, :, None, :], -1)
    token_len = jnp.sum(choose * lengths[:, :, None, :].astype(jnp.float32), -1)
    return (token_adv * SLOT / token_len).reshape(lengths.shape[0], -1)


def heads_of(rows):
    return rows.reshape(rows.shape[0], -1, HEAD_WIDTH).astype(jnp.float32)


def attend(query_rows, key_rows, value_rows, same_doc):
    keys, values = (heads_of(key_rows), heads_of(value_rows))
    count = keys.shape[1]
    queries = heads_of(query_rows).reshape(SLOT, count, -1, HEAD_WIDTH)
    scores = jnp.einsum("ikgd,jkd->kgij", queries, keys) * HEAD_WIDTH ** (-0.5)
    probs = jax.nn.softmax(jnp.where(same_doc, scores, masked_score), axis=-1)
    mixture = jnp.einsum("kgij,jkd->ikgd", probs.astype(jnp.bfloat16).astype(jnp.float32), values)
    return (mixture.reshape(SLOT, -1).astype(jnp.bfloat16), probs)


def attend_back(query_rows, key_rows, value_rows, probs, head_out_grad):
    keys, values = (heads_of(key_rows), heads_of(value_rows))
    count = keys.shape[1]
    queries = heads_of(query_rows).reshape(SLOT, count, -1, HEAD_WIDTH)
    grads = heads_of(head_out_grad).reshape(queries.shape)
    rounded = probs.astype(jnp.bfloat16).astype(jnp.float32)
    prob_grad = jnp.einsum("ikgd,jkd->kgij", grads, values)
    value_grad = jnp.einsum("kgij,ikgd->jkd", rounded, grads)
    score_grad = probs * (prob_grad - jnp.sum(prob_grad * probs, -1, keepdims=True))
    score_grad = score_grad.astype(jnp.bfloat16).astype(jnp.float32)
    scale = HEAD_WIDTH ** (-0.5)
    query_grad = jnp.einsum("kgij,jkd->ikgd", score_grad, keys) * scale
    key_grad = jnp.einsum("kgij,ikgd->jkd", score_grad, queries) * scale
    return jnp.concatenate(
        [v.reshape(SLOT, -1).astype(jnp.bfloat16) for v in (query_grad, key_grad, value_grad)], 1
    )


def dot(a, b, contract):
    return lax.dot_general(a, b, (contract, ((), ())), preferred_element_type=jnp.float32)


def scatter(value, axis):
    return lax.psum_scatter(value, axis, scatter_dimension=0, tiled=True)


def gather(value, axis):
    return lax.all_gather(value, axis, axis=0, tiled=True)


def local(
    inputs,
    head_grad,
    noise_mask,
    lengths,
    rewards,
    groups,
    query_weight,
    key_weight,
    value_weight,
    out_weight,
):
    core = lax.axis_index("pp")
    row_count = inputs.shape[1]
    query_cols, key_cols = (query_weight.shape[2], key_weight.shape[2])
    cols = query_cols + 2 * key_cols
    own_qkv = jnp.concatenate([query_weight[0], key_weight[0], value_weight[0]], 1)
    own_out = out_weight[0]
    swap = [(0, 1), (1, 0)]
    far_qkv, far_out = (lax.ppermute(own_qkv, "pp", swap), lax.ppermute(own_out, "pp", swap))
    qkv = [jnp.where(core == 0, own_qkv, far_qkv), jnp.where(core == 0, far_qkv, own_qkv)]
    out = [jnp.where(core == 0, own_out, far_out), jnp.where(core == 0, far_out, own_out)]
    segment = segments(lengths)[core, lax.axis_index("fsdp")]
    same_doc = segment[:, None] == segment[None, :]
    weight = lax.dynamic_slice_in_dim(
        token_weights(lengths, rewards, groups)[core],
        lax.axis_index("tp") * row_count,
        row_count,
        0,
    ) * noise_mask[core].astype(jnp.float32)
    top_grad = (-weight[:, None] * head_grad[core].astype(jnp.float32)).astype(jnp.bfloat16)

    def project(stream_all, layer):
        wide = stream_all.astype(jnp.float32)
        squares = jnp.sum(wide * wide, -1, keepdims=True)
        partial = jnp.concatenate(
            [
                dot(stream_all, qkv[layer], ((1,), (0,))),
                jnp.broadcast_to(squares, (squares.shape[0], 128)),
            ],
            1,
        )
        summed = scatter(partial, "fsdp")
        inv_rms = lax.rsqrt(summed[:, cols : cols + 1] / MODEL_WIDTH + epsilon)
        rows = (summed[:, :cols] * inv_rms).astype(jnp.bfloat16)
        return (
            inv_rms,
            rows[:, :query_cols],
            rows[:, query_cols : query_cols + key_cols],
            rows[:, query_cols + key_cols :],
        )

    def head_grads(grad_all, layer):
        return scatter(dot(grad_all, out[layer], ((1,), (1,))), "fsdp").astype(jnp.bfloat16)

    stream0 = inputs[core]
    stream0_all = gather(stream0, "tp")
    grad1_all = gather(top_grad, "tp")
    inv0, q0, k0, v0 = project(stream0_all, 0)
    head_grad1 = head_grads(grad1_all, 1)
    head0, probs0 = attend(q0, k0, v0, same_doc)
    heads0_all = gather(head0, "fsdp")
    stream1 = (
        stream0.astype(jnp.float32) + scatter(dot(heads0_all, out[0], ((1,), (0,))), "tp")
    ).astype(jnp.bfloat16)
    stream1_all = gather(stream1, "tp")
    inv1, q1, k1, v1 = project(stream1_all, 1)
    head1, probs1 = attend(q1, k1, v1, same_doc)
    heads1_all = gather(head1, "fsdp")
    grads1 = attend_back(q1, k1, v1, probs1, head_grad1).astype(jnp.float32)
    rows1 = jnp.concatenate([q1, k1, v1], 1).astype(jnp.float32)
    share = inv1 * jnp.sum(grads1 * rows1, -1, keepdims=True) * inv1 / MODEL_WIDTH
    scaled1 = (grads1 * inv1).astype(jnp.bfloat16)
    scaled1_all = gather(scaled1, "fsdp")
    share_all = gather(jnp.broadcast_to(share, (SLOT, 128)), "fsdp")[:, :1]
    part = dot(scaled1_all, qkv[1], ((1,), (1,))) - stream1_all.astype(jnp.float32) * share_all
    grad0 = (top_grad.astype(jnp.float32) + scatter(part, "tp")).astype(jnp.bfloat16)
    grad0_all = gather(grad0, "tp")
    head_grad0 = head_grads(grad0_all, 0)
    grads0 = attend_back(q0, k0, v0, probs0, head_grad0).astype(jnp.float32)
    scaled0_all = gather((grads0 * inv0).astype(jnp.bfloat16), "fsdp")

    def both(first, second):
        own = jnp.where(core == 0, first, second)
        other = lax.ppermute(jnp.where(core == 0, second, first), "pp", swap)
        return jnp.concatenate([own, other], 0)

    streams = both(stream0_all, stream1_all)
    heads = both(heads0_all, heads1_all)
    out_grads = both(grad0_all, grad1_all)
    scaled = both(scaled0_all, scaled1_all)
    qkv_grad = dot(streams, scaled, ((0,), (0,)))
    return (
        qkv_grad[None, :, :query_cols],
        qkv_grad[None, :, query_cols : query_cols + key_cols],
        qkv_grad[None, :, query_cols + key_cols :],
        dot(heads, out_grads, ((0,), (0,)))[None],
    )


def solution(mesh):
    return jax.shard_map(
        local,
        mesh=mesh,
        in_specs=(
            P(None, "tp", "fsdp"),
            P(None, "tp", "fsdp"),
            P(None, "tp"),
            P(),
            P(),
            P(),
            P("pp", "fsdp", "tp"),
            P("pp", "fsdp", "tp"),
            P("pp", "fsdp", "tp"),
            P("pp", "tp", "fsdp"),
        ),
        out_specs=(
            P("pp", "fsdp", "tp"),
            P("pp", "fsdp", "tp"),
            P("pp", "fsdp", "tp"),
            P("pp", "tp", "fsdp"),
        ),
        check_vma=False,
    )
```

profile of v0, /device:TPU:1, one launch (start us, length us, event | category | flops | bytes accessed | tf_op | source)
XLA Modules:
  0.0 620.1 jit_solution(6315300125879777344)
XLA Ops:
  7.2 1.6 pad_maximum_fusion.2
  8.8 1.5 collective-permute-start
  10.4 12.3 %all-gather = bf16[1,512,512]{2,1,0:T(8,128)(2,1)S(1)} all-gather(bf16[1,128,512]{2,1,0:T(8,128)(2,1)S(1)} %constant_dynamic-slice_fusion.2), channel_id=3, replica_groups=mesh['pp'=2,'fsdp'=16,'tp'=4] {'tp'}, dimensions={1}, use_global_device_ids=true | all-gather | bytes 655360 | tf_op jit(solution)/shard_map/all_gather | solution.py:81
  22.9 2.5 fusion.13
  25.5 2.0 pad_maximum_fusion
  27.5 0.6 copy-done.21
  28.4 76.2 %reduce-scatter.7.cloned.1.call-done = f32[32,1664]{1,0:T(8,128)} async-done(((f32[512,1664]{1,0:T(8,128)}), f32[32,1664]{1,0:T(8,128)}) %reduce-scatter.7.cloned.1.call-update) | async-done | bytes 213008 | tf_op jit(solution)/shard_map/reduce_scatter | solution.py:77
  104.6 0.8 fusion.78
  105.4 1.0 fusion.59
  106.8 0.6 copy-done.11
  107.7 0.7 convert_element_type.203
  108.5 2.5 collective-permute-start.1
  111.7 1.5 collective-permute-done.1
  113.2 37.5 %all-gather.7.cloned.1.call-done = bf16[512,1024]{1,0:T(8,128)(2,1)} async-done(((bf16[32,1024]{1,0:T(8,128)(2,1)}), bf16[512,1024]{1,0:T(8,128)(2,1)}) %all-gather.7.cloned.1.call-update) | async-done | bytes 1048592 | tf_op jit(solution)/shard_map/all_gather | solution.py:81
  150.7 2.9 fusion.53
  154.5 11.4 %all_gather.30 = bf16[512,512]{1,0:T(8,128)(2,1)S(1)} all-gather(bf16[128,512]{1,0:T(8,128)(2,1)S(1)} %fusion.54), channel_id=1, replica_groups=mesh['pp'=2,'fsdp'=16,'tp'=4] {'tp'}, dimensions={0}, use_global_device_ids=true | all-gather | bytes 655360 | tf_op jit(solution)/shard_map/all_gather | solution.py:81
  165.9 2.1 fusion.47
  168.1 9.5 %reduce-scatter.9.cloned.1.call-done = f32[128,512]{1,0:T(8,128)} async-done(((f32[512,512]{1,0:T(8,128)}), f32[128,512]{1,0:T(8,128)}) %reduce-scatter.9.cloned.1.call-update) | async-done | bytes 262160 | tf_op jit(solution)/shard_map/reduce_scatter | solution.py:77
  177.5 1.0 fusion.55
  178.5 10.3 %all_gather.29 = bf16[512,512]{1,0:T(8,128)(2,1)S(1)} all-gather(bf16[128,512]{1,0:T(8,128)(2,1)S(1)} %fusion.55), channel_id=1, replica_groups=mesh['pp'=2,'fsdp'=16,'tp'=4] {'tp'}, dimensions={0}, use_global_device_ids=true | all-gather | bytes 655360 | tf_op jit(solution)/shard_map/all_gather | solution.py:81
  189.0 2.3 fusion.50
  191.4 2.0 pad_maximum_fusion.1
  193.4 61.5 %reduce-scatter.13.cloned.1.call-done = f32[32,1024]{1,0:T(8,128)} async-done(((f32[512,1024]{1,0:T(8,128)}), f32[32,1024]{1,0:T(8,128)}) %reduce-scatter.13.cloned.1.call-update) | async-done | bytes 131088 | tf_op jit(solution)/shard_map/reduce_scatter | solution.py:77
  255.0 0.9 convert_element_type.216
  255.9 0.7 reshape.148
  256.6 77.0 %reduce-scatter.11.cloned.1.call-done = f32[32,1664]{1,0:T(8,128)} async-done(((f32[512,1664]{1,0:T(8,128)}), f32[32,1664]{1,0:T(8,128)}) %reduce-scatter.11.cloned.1.call-update) | async-done | bytes 213008 | tf_op jit(solution)/shard_map/reduce_scatter | solution.py:77
  333.5 0.9 fusion.87
  334.4 1.0 fusion.58
  335.5 0.6 slice.70
  336.1 0.9 reshape.146
  337.0 1.6 fusion.128
  338.6 1.2 multiply_reduce_fusion.2
  339.8 0.9 multiply_convert_fusion.2
  340.9 0.4 fusion.39
  341.3 1.9 fusion.38
  343.2 0.7 convert_element_type.220
  343.9 0.7 copy.219
  344.6 1.7 fusion.57
  346.4 1.2 dynamic-slice.1
  348.8 30.9 %all-reduce = f32[512]{0:T(512)S(1)} all-reduce(f32[512]{0:T(512)S(1)} %dynamic-update-slice), channel_id=4, replica_groups=mesh['pp'=2,'fsdp'=16,'tp'=4] {'fsdp'}, use_global_device_ids=true, to_apply=%add | all-reduce | flops 512 | bytes 4096
  379.7 10.6 %all-gather.9.cloned.1.call-done = bf16[512,1536]{1,0:T(8,128)(2,1)} async-done(((bf16[32,1536]{1,0:T(8,128)(2,1)}), bf16[512,1536]{1,0:T(8,128)(2,1)}) %all-gather.9.cloned.1.call-update) | async-done | bytes 1572880 | tf_op jit(solution)/shard_map/all_gather | solution.py:81
  390.4 3.7 convolution_subtract_fusion
  394.1 22.9 %reduce-scatter.15.cloned.1.call-done = f32[128,512]{1,0:T(8,128)} async-done(((f32[512,512]{1,0:T(8,128)}), f32[128,512]{1,0:T(8,128)}) %reduce-scatter.15.cloned.1.call-update) | async-done | bytes 262160 | tf_op jit(solution)/shard_map/reduce_scatter | solution.py:77
  417.0 1.1 add_convert_fusion
  418.1 11.1 %all_gather.33 = bf16[512,512]{1,0:T(8,128)(2,1)S(1)} all-gather(bf16[128,512]{1,0:T(8,128)(2,1)S(1)} %add_convert_fusion), channel_id=1, replica_groups=mesh['pp'=2,'fsdp'=16,'tp'=4] {'tp'}, dimensions={0}, use_global_device_ids=true | all-gather | bytes 655360 | tf_op jit(solution)/shard_map/all_gather | solution.py:81
  429.2 3.3 fusion.52
  432.6 74.5 %reduce-scatter.17.cloned.1.call-done = f32[32,1024]{1,0:T(8,128)} async-done(((f32[512,1024]{1,0:T(8,128)}), f32[32,1024]{1,0:T(8,128)}) %reduce-scatter.17.cloned.1.call-update) | async-done | bytes 131088 | tf_op jit(solution)/shard_map/reduce_scatter | solution.py:77
  507.1 0.9 convert_element_type.232
  508.9 0.4 fusion.36
  509.4 0.7 multiply_convert_fusion
  510.5 0.7 convert_element_type.247
  511.2 43.0 %all-gather.11.cloned.1.call-done = bf16[512,1536]{1,0:T(8,128)(2,1)} async-done(((bf16[32,1536]{1,0:T(8,128)(2,1)}), bf16[512,1536]{1,0:T(8,128)(2,1)}) %all-gather.11.cloned.1.call-update) | async-done | bytes 1572880 | tf_op jit(solution)/shard_map/all_gather | solution.py:81
  554.2 3.8 broadcast_select_fusion.1
  557.9 1.6 collective-permute-start.3
  559.6 38.7 %all-gather.13.cloned.1.call-done = bf16[512,1024]{1,0:T(8,128)(2,1)} async-done(((bf16[32,1024]{1,0:T(8,128)(2,1)}), bf16[512,1024]{1,0:T(8,128)(2,1)}) %all-gather.13.cloned.1.call-update) | async-done | bytes 1048592 | tf_op jit(solution)/shard_map/all_gather | solution.py:81
  598.3 1.4 broadcast_select_fusion.4
  599.6 2.2 collective-permute-start.4
  602.1 0.8 collective-permute-start.2
  602.8 1.3 collective-permute-done.4
  604.1 0.7 collective-permute-done.5
  604.9 2.6 fusion.10
  607.5 3.3 fusion.2
  610.7 1.5 slice_bitcast_fusion
  612.2 1.0 slice_bitcast_fusion.1
  (151 shorter events, 5.8 us)
Async XLA Ops:
  7.2 3.2 copy-start.8
  7.2 97.4 %reduce-scatter.7.cloned.1.call-start = ((), (), s32[]{:S(2)}) async-start(), calls=%async_computation.6 | async-start | bytes 3620864 | tf_op jit(solution)/shard_map/reduce_scatter | solution.py:77
  7.2 15.6 %copy-start.3 = (bf16[1,512,1024]{2,1,0:T(8,128)(2,1)S(1)}, bf16[1,512,1024]{2,1,0:T(8,128)(2,1)}, u32[]{:S(2)}) copy-start(bf16[1,512,1024]{2,1,0:T(8,128)(2,1)} %param.16) | copy-start | bytes 3145732
  7.2 15.6 %copy-start.6 = (bf16[1,512,256]{2,1,0:T(8,128)(2,1)S(1)}, bf16[1,512,256]{2,1,0:T(8,128)(2,1)}, u32[]{:S(2)}) copy-start(bf16[1,512,256]{2,1,0:T(8,128)(2,1)} %param.18) | copy-start | bytes 786436
  8.8 14.0 %collective-permute-start = (bf16[512,1536]{1,0:T(8,128)(2,1)S(1)}, bf16[512,1536]{1,0:T(8,128)(2,1)}, u32[]{:S(2)}, u32[]{:S(2)}) collective-permute-start(bf16[512,1536]{1,0:T(8,128)(2,1)S(1)} %pad_maximum_fusion.2), channel_id=1, source_target_pairs={{0,64},{64,0},{1,65},{65,1},{2,66},{66,2},{3,67},{67,3},{4,68},{68... | collective-permute-start | bytes 4718600 | tf_op jit(solution)/shard_map/ppermute | solution.py:103
  27.4 0.7 copy-start.21
  27.4 0.8 slice-start
  27.4 81.0 %copy-start = (bf16[1,1024,512]{2,1,0:T(8,128)(2,1)S(1)}, bf16[1,1024,512]{2,1,0:T(8,128)(2,1)}, u32[]{:S(2)}) copy-start(bf16[1,1024,512]{2,1,0:T(8,128)(2,1)} %param.19) | copy-start | bytes 3145732
  27.4 83.5 %copy-start.29 = (s32[2,16,2]{1,2,0:T(2,128)S(1)}, s32[2,16,2]{1,2,0:T(2,128)}, u32[]{:S(2)}) copy-start(s32[2,16,2]{1,2,0:T(2,128)} %param.15) | copy-start | bytes 772
  27.5 83.7 %copy-start.30 = (s32[2,16,2]{1,2,0:T(2,128)S(1)}, s32[2,16,2]{1,2,0:T(2,128)}, u32[]{:S(2)}) copy-start(s32[2,16,2]{1,2,0:T(2,128)} %param.14) | copy-start | bytes 772
  27.5 123.2 %all-gather.7.cloned.1.call-start = ((), (), s32[]{:S(2)}) async-start(), calls=%async_computation.7 | async-start | bytes 1114112 | tf_op jit(solution)/shard_map/all_gather | solution.py:81
  28.4 78.5 %copy-start.28 = (pred[32,32]{0,1:T(8,128)(4,1)}, pred[32,32]{0,1:T(8,128)(4,1)S(1)}, u32[]{:S(2)}) copy-start(pred[32,32]{0,1:T(8,128)(4,1)S(1)} %broadcast_compare_fusion) | copy-start | bytes 3076
  105.4 48.2 %copy-start.18 = (f32[32]{0:T(128)}, f32[32]{0:T(128)S(1)}, u32[]{:S(2)}) copy-start(f32[32]{0:T(128)S(1)} %fusion.78) | copy-start | bytes 388
  106.5 5.1 copy-start.14
  106.8 0.7 copy-start.11
  106.8 4.9 copy-start.24
  108.4 69.1 %reduce-scatter.9.cloned.1.call-start = ((), (), s32[]{:S(2)}) async-start(), calls=%async_computation.8 | async-start | bytes 1310720 | tf_op jit(solution)/shard_map/reduce_scatter | solution.py:77
  108.5 4.8 collective-permute-start.1
  111.7 42.6 %copy-start.31 = (s32[2,128]{1,0:T(2,128)S(1)}, s32[2,128]{1,0:T(2,128)}, u32[]{:S(2)}) copy-start(s32[2,128]{1,0:T(2,128)} %param.12) | copy-start | bytes 3076
  111.7 42.7 %copy-start.10 = (bf16[2,128,512]{2,1,0:T(8,128)(2,1)S(1)}, bf16[2,128,512]{2,1,0:T(8,128)(2,1)}, u32[]{:S(2)}) copy-start(bf16[2,128,512]{2,1,0:T(8,128)(2,1)} %param.11) | copy-start | bytes 786436
  113.2 52.7 %copy-start.1 = (bf16[1024,512]{1,0:T(8,128)(2,1)}, bf16[1024,512]{1,0:T(8,128)(2,1)S(1)}, u32[]{:S(2)}) copy-start(bf16[1024,512]{1,0:T(8,128)(2,1)S(1)} %collective-permute-done.1) | copy-start | bytes 3145732
  153.7 101.3 %reduce-scatter.13.cloned.1.call-start = ((), (), s32[]{:S(2)}) async-start(), calls=%async_computation.10 | async-start | bytes 2228224 | tf_op jit(solution)/shard_map/reduce_scatter | solution.py:77
  154.4 13.5 %copy-start.22 = (f32[128]{0:T(128)}, f32[128]{0:T(128)S(1)}, u32[]{:S(2)}) copy-start(f32[128]{0:T(128)S(1)} %fusion.100) | copy-start | bytes 1540
  168.0 9.6 %copy-start.9 = (bf16[2,128,512]{2,1,0:T(8,128)(2,1)S(1)}, bf16[2,128,512]{2,1,0:T(8,128)(2,1)}, u32[]{:S(2)}) copy-start(bf16[2,128,512]{2,1,0:T(8,128)(2,1)} %param.10) | copy-start | bytes 786436
  168.0 21.0 %copy-start.7 = (bf16[1,512,256]{2,1,0:T(8,128)(2,1)S(1)}, bf16[1,512,256]{2,1,0:T(8,128)(2,1)}, u32[]{:S(2)}) copy-start(bf16[1,512,256]{2,1,0:T(8,128)(2,1)} %param.17) | copy-start | bytes 786436
  168.0 165.5 %reduce-scatter.11.cloned.1.call-start = ((), (), s32[]{:S(2)}) async-start(), calls=%async_computation.9 | async-start | bytes 3620864 | tf_op jit(solution)/shard_map/reduce_scatter | solution.py:77
  193.4 197.0 %all-gather.9.cloned.1.call-start = ((), (), s32[]{:S(2)}) async-start(), calls=%async_computation.11 | async-start | bytes 1671168 | tf_op jit(solution)/shard_map/all_gather | solution.py:81
  333.5 11.1 %copy-start.5 = (f32[32,1664]{1,0:T(8,128)S(1)}, f32[32,1664]{1,0:T(8,128)}, u32[]{:S(2)}) copy-start(f32[32,1664]{1,0:T(8,128)} %reduce-scatter.11.cloned.1.call-done) | copy-start | bytes 638980
  334.4 2.5 copy-start.20
  337.0 57.0 %copy-start.16 = (bf16[32,2,128]{2,1,0:T(2,128)(2,1)}, bf16[32,2,128]{2,1,0:T(2,128)(2,1)S(1)}, u32[]{:S(2)}) copy-start(bf16[32,2,128]{2,1,0:T(2,128)(2,1)S(1)} %reshape.147) | copy-start | bytes 49156
  338.6 4.6 copy-start.26
  346.4 70.7 %reduce-scatter.15.cloned.1.call-start = ((), (), s32[]{:S(2)}) async-start(), calls=%async_computation.12 | async-start | bytes 1310720 | tf_op jit(solution)/shard_map/reduce_scatter | solution.py:77
  379.7 37.3 %copy-start.23 = (f32[128]{0:T(128)S(1)}, f32[128]{0:T(128)}, u32[]{:S(2)}) copy-start(f32[128]{0:T(128)} %copy-done.22) | copy-start | bytes 1540
  394.1 113.0 %reduce-scatter.17.cloned.1.call-start = ((), (), s32[]{:S(2)}) async-start(), calls=%async_computation.13 | async-start | bytes 2228224 | tf_op jit(solution)/shard_map/reduce_scatter | solution.py:77
  432.5 75.6 %copy-start.12 = (f32[2,4,32,32]{2,3,1,0:T(8,128)S(1)}, f32[2,4,32,32]{2,3,1,0:T(8,128)}, u32[]{:S(2)}) copy-start(f32[2,4,32,32]{2,3,1,0:T(8,128)} %copy-done.11) | copy-start | bytes 98308
  432.5 75.6 %copy-start.15 = (bf16[32,2,128]{2,1,0:T(2,128)(2,1)S(1)}, bf16[32,2,128]{2,1,0:T(2,128)(2,1)}, u32[]{:S(2)}) copy-start(bf16[32,2,128]{2,1,0:T(2,128)(2,1)} %copy-done.14) | copy-start | bytes 49156
  432.5 75.6 %copy-start.25 = (f32[2,4,32]{2,1,0:T(4,128)S(1)}, f32[2,4,32]{2,1,0:T(4,128)}, u32[]{:S(2)}) copy-start(f32[2,4,32]{2,1,0:T(4,128)} %copy-done.24) | copy-start | bytes 3076
  432.5 76.9 %copy-start.19 = (f32[32]{0:T(128)S(1)}, f32[32]{0:T(128)}, u32[]{:S(2)}) copy-start(f32[32]{0:T(128)} %copy-done.18) | copy-start | bytes 388
  432.5 77.8 %copy-start.13 = (f32[2,4,32,32]{2,3,1,0:T(8,128)S(1)}, f32[2,4,32,32]{2,3,1,0:T(8,128)}, u32[]{:S(2)}) copy-start(f32[2,4,32,32]{2,3,1,0:T(8,128)} %get-tuple-element.29) | copy-start | bytes 98308
  432.5 77.7 %copy-start.17 = (bf16[32,2,128]{2,1,0:T(2,128)(2,1)S(1)}, bf16[32,2,128]{2,1,0:T(2,128)(2,1)}, u32[]{:S(2)}) copy-start(bf16[32,2,128]{2,1,0:T(2,128)(2,1)} %copy-done.16) | copy-start | bytes 49156
  432.5 77.7 %copy-start.27 = (f32[2,4,32]{2,1,0:T(4,128)S(1)}, f32[2,4,32]{2,1,0:T(4,128)}, u32[]{:S(2)}) copy-start(f32[2,4,32]{2,1,0:T(4,128)} %copy-done.26) | copy-start | bytes 3076
  432.5 121.6 %all-gather.11.cloned.1.call-start = ((), (), s32[]{:S(2)}) async-start(), calls=%async_computation.14 | async-start | bytes 1671168 | tf_op jit(solution)/shard_map/all_gather | solution.py:81
  510.2 88.1 %all-gather.13.cloned.1.call-start = ((), (), s32[]{:S(2)}) async-start(), calls=%async_computation.15 | async-start | bytes 1114112 | tf_op jit(solution)/shard_map/all_gather | solution.py:81
  511.2 87.1 %copy-start.4 = (bf16[512,1024]{1,0:T(8,128)(2,1)S(1)}, bf16[512,1024]{1,0:T(8,128)(2,1)}, u32[]{:S(2)}) copy-start(bf16[512,1024]{1,0:T(8,128)(2,1)} %all-gather.7.cloned.1.call-done) | copy-start | bytes 3145732
  557.9 49.5 %collective-permute-start.3 = (bf16[512,1536]{1,0:T(8,128)(2,1)}, bf16[512,1536]{1,0:T(8,128)(2,1)}, u32[]{:S(2)}, u32[]{:S(2)}) collective-permute-start(bf16[512,1536]{1,0:T(8,128)(2,1)} %get-tuple-element.11), channel_id=1, source_target_pairs={{0,64},{64,0},{1,65},{65,1},{2,66},{66,2},{3,67},{67,3},{4,68},{68... | collective-permute-start | bytes 4718600 | tf_op jit(solution)/shard_map/ppermute | solution.py:168
  599.6 4.5 collective-permute-start.4
  601.9 3.0 collective-permute-start.5
  602.1 5.4 collective-permute-start.2
  604.9 2.6 copy-start.2
Sparse Core Ops, SparseCore 0:
  27.6 76.9 reduce-scatter.6
  108.5 42.1 all-gather.6
  153.8 23.7 reduce-scatter.8
  181.6 73.3 reduce-scatter.12
  258.2 75.3 reduce-scatter.10
  346.5 43.8 all-gather.8
  394.2 22.7 reduce-scatter.14
  432.7 74.4 reduce-scatter.16
  510.3 43.8 all-gather.10
  556.7 41.4 all-gather.12
where the time goes:
time: 621 us; the launch traced here: 620 us
  waiting for transfers between devices  455 us (73%)
  blocking collectives  76 us (12%)
  matrix products  29.6 us (5%)
  other arithmetic  23.1 us (4%)
  between operations  15.4 us (2%)
  local copies, waits for them, and re-layouts  11.7 us (2%)
  starting transfers between devices  9.02 us (1%)
    reduce_scatter x6, waiting for transfers between devices, scatter(): return lax.psum_scatter(value, axis, scatter_dimension=0, tiled=True)  322 us
    all_gather x4, waiting for transfers between devices, gather(): return lax.all_gather(value, axis, axis=0, tiled=True)  130 us
    all_gather x4, blocking collectives, gather(): return lax.all_gather(value, axis, axis=0, tiled=True)  45 us
    unnamed x1, blocking collectives  30.9 us
    dot_general x8, matrix products, dot(): lax.dot_general(a, b, (contract, ((), ())), preferred_element_type=jnp.fl...  22.5 us
  transfers between devices with their start and end apart: 16, of which 13 were waited for; matrix products, arithmetic and copies ran while one was open for 3% of the time, Pallas kernels for 0%

commit v1 on v0

--- a/solution.py
+++ b/solution.py
@@ -8,6 +8,13 @@
 SLOT = 32
 epsilon = 1e-06
 masked_score = -1e30
+
+
+def all_by_exchange(x, axis, dim):
+    peers = lax.axis_size(axis)
+    blocks = jnp.stack([x for _ in range(peers)])
+    blocks = lax.all_to_all(blocks, axis, split_axis=0, concat_axis=0)
+    return jnp.concatenate(blocks, axis=dim)
 
 
 def segments(lengths):
@@ -78,7 +85,7 @@
 
 
 def gather(value, axis):
-    return lax.all_gather(value, axis, axis=0, tiled=True)
+    return all_by_exchange(value, axis, 0)
 
 
 def local(

time: 621 us -> 543 us (0.87)
  waiting for transfers between devices: 455 us -> 384 us
  blocking collectives: 76 us -> 48.3 us
  starting transfers between devices: 9.02 us -> 35 us
  matrix products: 29.6 us -> 20.5 us
    all_gather x4 -> x0, waiting for transfers between devices: 130 us -> none  [gather(): return lax.all_gather(value, axis, axis=0, tiled=True)]
    all_to_all x0 -> x5, waiting for transfers between devices: none -> 71.1 us  [all_by_exchange(): blocks = lax.all_to_all(blocks, axis, split_axis=0, concat_axis=0)]
    all_to_all x0 -> x4, blocking collectives: none -> 48.3 us  [all_by_exchange(): blocks = lax.all_to_all(blocks, axis, split_axis=0, concat_axis=0)]
    all_gather x4 -> x0, blocking collectives: 45 us -> none  [gather(): return lax.all_gather(value, axis, axis=0, tiled=True)]
    unnamed x1 -> x0, blocking collectives: 30.9 us -> none
    all_to_all x0 -> x5, starting transfers between devices: none -> 24 us  [all_by_exchange(): blocks = lax.all_to_all(blocks, axis, split_axis=0, concat_axis=0)]
    reduce_scatter x6, waiting for transfers between devices: 322 us -> 312 us  [scatter(): return lax.psum_scatter(value, axis, scatter_dimension=0, tiled=True)]
  transfers between devices with their start and end apart: 16 -> 17, of which waited for: 13 -> 13; matrix products, arithmetic and copies ran while one was open for 3% -> 5% of each run, Pallas kernels for 0% -> 0%
where the time goes in v1:
time: 543 us; the launch traced here: 541 us
  waiting for transfers between devices  384 us (71%)
  blocking collectives  48.3 us (9%)
  starting transfers between devices  35 us (6%)
  other arithmetic  22.9 us (4%)
  matrix products  20.5 us (4%)
  local copies, waits for them, and re-layouts  15.5 us (3%)
  between operations  14.8 us (3%)
    reduce_scatter x6, waiting for transfers between devices, scatter(): return lax.psum_scatter(value, axis, scatter_dimension=0, tiled=True)  312 us
    all_to_all x5, waiting for transfers between devices, all_by_exchange(): blocks = lax.all_to_all(blocks, axis, split_axis=0, concat_axis=0)  71.1 us
    all_to_all x4, blocking collectives, all_by_exchange(): blocks = lax.all_to_all(blocks, axis, split_axis=0, concat_axis=0)  48.3 us
    all_to_all x5, starting transfers between devices, all_by_exchange(): blocks = lax.all_to_all(blocks, axis, split_axis=0, concat_axis=0)  24 us
    dot_general x8, matrix products, dot(): lax.dot_general(a, b, (contract, ((), ())), preferred_element_type=jnp.fl...  17.2 us
  transfers between devices with their start and end apart: 17, of which 13 were waited for; matrix products, arithmetic and copies ran while one was open for 5% of the time, Pallas kernels for 0%

profile of v1, /device:TPU:1, one launch (start us, length us, event | category | flops | bytes accessed | tf_op | source)
XLA Modules:
  0.0 541.5 jit_solution(14457810378640062822)
XLA Ops:
  7.2 1.6 pad_maximum_fusion.2
  8.8 1.5 collective-permute-start
  10.3 0.8 stack.24
  11.2 5.1 all-to-all-start
  16.3 9.3 %all-to-all-done = bf16[4,128,512]{2,1,0:T(8,128)(2,1)S(1)} async-done(((bf16[4,128,512]{2,1,0:T(8,128)(2,1)}), bf16[4,128,512]{2,1,0:T(8,128)(2,1)S(1)}, u32[]{:S(2)}, u32[]{:S(2)}) %all-to-all-start) | async-done | bytes 524320 | tf_op jit(solution)/shard_map/all_to_all | solution.py:16
  25.8 2.4 fusion.13
  28.4 2.0 pad_maximum_fusion
  30.4 1.2 copy-done.8
  31.6 0.7 collective-permute-start.1
  33.0 71.4 %reduce-scatter.7.cloned.1.call-done = f32[32,1664]{1,0:T(8,128)} async-done(((f32[512,1664]{1,0:T(8,128)}), f32[32,1664]{1,0:T(8,128)}) %reduce-scatter.7.cloned.1.call-update) | async-done | bytes 213008 | tf_op jit(solution)/shard_map/reduce_scatter | solution.py:84
  104.4 0.8 fusion.78
  105.8 1.0 fusion.58
  108.1 1.1 stack.27
  109.2 4.7 all-to-all-start.1
  114.9 14.0 %all-to-all-done.1 = bf16[16,32,1024]{2,1,0:T(8,128)(2,1)S(1)} async-done(((bf16[16,32,1024]{2,1,0:T(8,128)(2,1)}), bf16[16,32,1024]{2,1,0:T(8,128)(2,1)S(1)}, u32[]{:S(2)}, u32[]{:S(2)}) %all-to-all-start.1) | async-done | bytes 1048608 | tf_op jit(solution)/shard_map/all_to_all | solution.py:16
  128.9 1.7 fusion.51
  131.3 0.7 max.15
  132.0 0.6 subtract_divide_fusion
  132.6 0.8 copy.123
  133.4 0.8 select_reduce_fusion.1
  134.3 0.8 fusion.100
  135.1 1.0 fusion.59
  136.1 17.6 %all_to_all.45 = bf16[4,128,512]{2,1,0:T(8,128)(2,1)S(1)} all-to-all(bf16[4,128,512]{2,1,0:T(8,128)(2,1)S(1)} %stack.30), channel_id=1, replica_groups=mesh['pp'=2,'fsdp'=16,'tp'=4] {'tp'}, dimensions={0} | all-to-all | bytes 1048576 | tf_op jit(solution)/shard_map/all_to_all | solution.py:16
  153.7 0.8 copy-done
  154.5 2.1 fusion.46
  156.6 1.2 reduce-scatter.9.cloned.1.call-done
  157.8 1.0 add_convert_fusion.1
  158.8 9.3 %all_to_all.46 = bf16[4,128,512]{2,1,0:T(8,128)(2,1)S(1)} all-to-all(bf16[4,128,512]{2,1,0:T(8,128)(2,1)S(1)} %stack.28), channel_id=1, replica_groups=mesh['pp'=2,'fsdp'=16,'tp'=4] {'tp'}, dimensions={0} | all-to-all | bytes 1048576 | tf_op jit(solution)/shard_map/all_to_all | solution.py:16
  168.4 1.0 fusion.49
  169.5 2.0 pad_maximum_fusion.1
  171.5 61.9 %reduce-scatter.13.cloned.1.call-done = f32[32,1024]{1,0:T(8,128)} async-done(((f32[512,1024]{1,0:T(8,128)}), f32[32,1024]{1,0:T(8,128)}) %reduce-scatter.13.cloned.1.call-update) | async-done | bytes 131088 | tf_op jit(solution)/shard_map/reduce_scatter | solution.py:84
  233.4 0.9 convert_element_type.240
  234.4 77.6 %reduce-scatter.11.cloned.1.call-done = f32[32,1664]{1,0:T(8,128)} async-done(((f32[512,1664]{1,0:T(8,128)}), f32[32,1664]{1,0:T(8,128)}) %reduce-scatter.11.cloned.1.call-update) | async-done | bytes 213008 | tf_op jit(solution)/shard_map/reduce_scatter | solution.py:84
  312.0 0.9 fusion.87
  312.9 1.0 fusion.57
  316.1 12.0 %all_to_all.47 = f32[16,32,128]{2,1,0:T(8,128)S(1)} all-to-all(f32[16,32,128]{2,1,0:T(8,128)S(1)} %stack.32), channel_id=1, replica_groups=mesh['pp'=2,'fsdp'=16,'tp'=4] {'fsdp'}, dimensions={0} | all-to-all | bytes 524288 | tf_op jit(solution)/shard_map/all_to_all | solution.py:16
  328.2 1.3 stack.31
  329.5 3.7 all-to-all-start.4
  333.4 19.4 %all-to-all-done.4 = bf16[16,32,1536]{2,1,0:T(8,128)(2,1)S(1)} async-done(((bf16[16,32,1536]{2,1,0:T(8,128)(2,1)}), bf16[16,32,1536]{2,1,0:T(8,128)(2,1)S(1)}, u32[]{:S(2)}, u32[]{:S(2)}) %all-to-all-start.4) | async-done | bytes 1572896 | tf_op jit(solution)/shard_map/all_to_all | solution.py:16
  352.7 3.4 convolution_subtract_fusion
  356.2 24.1 %reduce-scatter.15.cloned.1.call-done = f32[128,512]{1,0:T(8,128)} async-done(((f32[512,512]{1,0:T(8,128)}), f32[128,512]{1,0:T(8,128)}) %reduce-scatter.15.cloned.1.call-update) | async-done | bytes 262160 | tf_op jit(solution)/shard_map/reduce_scatter | solution.py:84
  380.3 1.1 add_convert_fusion
  381.5 9.3 %all_to_all.48 = bf16[4,128,512]{2,1,0:T(8,128)(2,1)S(1)} all-to-all(bf16[4,128,512]{2,1,0:T(8,128)(2,1)S(1)} %stack.33), channel_id=1, replica_groups=mesh['pp'=2,'fsdp'=16,'tp'=4] {'tp'}, dimensions={0} | all-to-all | bytes 1048576 | tf_op jit(solution)/shard_map/all_to_all | solution.py:16
  390.8 0.8 copy-done.2
  391.6 2.1 fusion.50
  393.7 75.4 %reduce-scatter.17.cloned.1.call-done = f32[32,1024]{1,0:T(8,128)} async-done(((f32[512,1024]{1,0:T(8,128)}), f32[32,1024]{1,0:T(8,128)}) %reduce-scatter.17.cloned.1.call-update) | async-done | bytes 131088 | tf_op jit(solution)/shard_map/reduce_scatter | solution.py:84
  469.1 0.9 convert_element_type.257
  471.6 1.3 stack.34
  472.9 4.4 all-to-all-start.7
  477.6 19.5 %all-to-all-done.7 = bf16[16,32,1536]{2,1,0:T(8,128)(2,1)S(1)} async-done(((bf16[16,32,1536]{2,1,0:T(8,128)(2,1)}), bf16[16,32,1536]{2,1,0:T(8,128)(2,1)S(1)}, u32[]{:S(2)}, u32[]{:S(2)}) %all-to-all-start.7) | async-done | bytes 1572896 | tf_op jit(solution)/shard_map/all_to_all | solution.py:16
  497.1 1.1 stack.35
  498.2 6.0 %all-to-all-start.8 = ((bf16[16,32,1024]{2,1,0:T(8,128)(2,1)}), bf16[16,32,1024]{2,1,0:T(8,128)(2,1)}, u32[]{:S(2)}, u32[]{:S(2)}) async-start(bf16[16,32,1024]{2,1,0:T(8,128)(2,1)} %stack.35), calls=%async_computation.14 | async-start | bytes 2097152 | tf_op jit(solution)/shard_map/all_to_all | solution.py:16
  504.2 2.1 bitcast_select_fusion.1
  506.3 3.3 collective-permute-start.3
  509.6 8.9 %all-to-all-done.8 = bf16[16,32,1024]{2,1,0:T(8,128)(2,1)} async-done(((bf16[16,32,1024]{2,1,0:T(8,128)(2,1)}), bf16[16,32,1024]{2,1,0:T(8,128)(2,1)}, u32[]{:S(2)}, u32[]{:S(2)}) %all-to-all-start.8) | async-done | bytes 1048608 | tf_op jit(solution)/shard_map/all_to_all | solution.py:16
  518.5 1.7 bitcast_select_fusion.3
  520.2 4.4 collective-permute-start.4
  525.0 0.9 collective-permute-start.2
  525.9 1.0 collective-permute-done.4
  526.9 0.7 collective-permute-done.5
  527.6 2.6 fusion.10
  530.2 1.9 fusion.2
  532.1 1.5 slice_bitcast_fusion
  533.6 1.0 slice_bitcast_fusion.1
  (163 shorter events, 9.6 us)
Async XLA Ops:
  7.2 3.1 copy-start.18
  7.2 18.6 %copy-start.13 = (bf16[1,512,1024]{2,1,0:T(8,128)(2,1)S(1)}, bf16[1,512,1024]{2,1,0:T(8,128)(2,1)}, u32[]{:S(2)}) copy-start(bf16[1,512,1024]{2,1,0:T(8,128)(2,1)} %param.16) | copy-start | bytes 3145732
  7.2 18.6 %copy-start.16 = (bf16[1,512,256]{2,1,0:T(8,128)(2,1)S(1)}, bf16[1,512,256]{2,1,0:T(8,128)(2,1)}, u32[]{:S(2)}) copy-start(bf16[1,512,256]{2,1,0:T(8,128)(2,1)} %param.18) | copy-start | bytes 786436
  8.8 16.9 %collective-permute-start = (bf16[512,1536]{1,0:T(8,128)(2,1)S(1)}, bf16[512,1536]{1,0:T(8,128)(2,1)}, u32[]{:S(2)}, u32[]{:S(2)}) collective-permute-start(bf16[512,1536]{1,0:T(8,128)(2,1)S(1)} %pad_maximum_fusion.2), channel_id=1, source_target_pairs={{0,64},{64,0},{1,65},{65,1},{2,66},{66,2},{3,67},{67,3},{4,68},{68... | collective-permute-start | bytes 4718600 | tf_op jit(solution)/shard_map/ppermute | solution.py:110
  11.2 14.4 %all-to-all-start = ((bf16[4,128,512]{2,1,0:T(8,128)(2,1)}), bf16[4,128,512]{2,1,0:T(8,128)(2,1)S(1)}, u32[]{:S(2)}, u32[]{:S(2)}) async-start(bf16[4,128,512]{2,1,0:T(8,128)(2,1)} %stack.24), calls=%async_computation | async-start | bytes 1048576 | tf_op jit(solution)/shard_map/all_to_all | solution.py:16
  16.3 88.2 %reduce-scatter.7.cloned.1.call-start = ((), (), s32[]{:S(2)}) async-start(), calls=%async_computation.15 | async-start | bytes 3620864 | tf_op jit(solution)/shard_map/reduce_scatter | solution.py:84
  25.6 2.7 copy-start.4
  30.3 1.2 copy-start.8
  30.3 1.9 copy-start.29
  30.3 2.5 slice-start
  31.6 83.3 %collective-permute-start.1 = (bf16[1024,512]{1,0:T(8,128)(2,1)S(1)}, bf16[1024,512]{1,0:T(8,128)(2,1)S(1)}, u32[]{:S(2)}, u32[]{:S(2)}) collective-permute-start(bf16[1024,512]{1,0:T(8,128)(2,1)S(1)} %bitcast.182), channel_id=1, source_target_pairs={{0,64},{64,0},{1,65},{65,1},{2,66},{66,2},{3,67},{67,3},{4,68},{68... | collective-permute-start | bytes 3145736 | tf_op jit(solution)/shard_map/ppermute | solution.py:110
  33.0 74.2 %copy-start.32 = (pred[32,32]{0,1:T(8,128)(4,1)}, pred[32,32]{0,1:T(8,128)(4,1)S(1)}, u32[]{:S(2)}) copy-start(pred[32,32]{0,1:T(8,128)(4,1)S(1)} %broadcast_compare_fusion) | copy-start | bytes 3076
  105.3 0.5 copy-start.27
  106.9 2.3 copy-start.25
  106.9 7.1 %copy-start.34 = (s32[2,16,2]{1,2,0:T(2,128)S(1)}, s32[2,16,2]{1,2,0:T(2,128)}, u32[]{:S(2)}) copy-start(s32[2,16,2]{1,2,0:T(2,128)} %param.15) | copy-start | bytes 772
  106.9 7.3 %copy-start.35 = (s32[2,16,2]{1,2,0:T(2,128)S(1)}, s32[2,16,2]{1,2,0:T(2,128)}, u32[]{:S(2)}) copy-start(s32[2,16,2]{1,2,0:T(2,128)} %param.14) | copy-start | bytes 772
  107.2 0.6 copy-start.21
  107.2 6.8 %copy-start.30 = (f32[2,4,32]{2,1,0:T(4,128)}, f32[2,4,32]{2,1,0:T(4,128)S(1)}, u32[]{:S(2)}) copy-start(f32[2,4,32]{2,1,0:T(4,128)S(1)} %get-tuple-element.26) | copy-start | bytes 3076
  109.2 19.7 %all-to-all-start.1 = ((bf16[16,32,1024]{2,1,0:T(8,128)(2,1)}), bf16[16,32,1024]{2,1,0:T(8,128)(2,1)S(1)}, u32[]{:S(2)}, u32[]{:S(2)}) async-start(bf16[16,32,1024]{2,1,0:T(8,128)(2,1)} %stack.27), calls=%async_computation.2 | async-start | bytes 2097152 | tf_op jit(solution)/shard_map/all_to_all | solution.py:16
  113.9 43.9 %reduce-scatter.9.cloned.1.call-start = ((), (), s32[]{:S(2)}) async-start(), calls=%async_computation.16 | async-start | bytes 1310720 | tf_op jit(solution)/shard_map/reduce_scatter | solution.py:84
  114.9 38.8 %copy-start.9 = (bf16[1024,512]{1,0:T(8,128)(2,1)}, bf16[1024,512]{1,0:T(8,128)(2,1)S(1)}, u32[]{:S(2)}) copy-start(bf16[1024,512]{1,0:T(8,128)(2,1)S(1)} %collective-permute-done.1) | copy-start | bytes 3145732
  128.9 27.7 %copy-start.11 = (bf16[16,32,1024]{2,1,0:T(8,128)(2,1)}, bf16[16,32,1024]{2,1,0:T(8,128)(2,1)S(1)}, u32[]{:S(2)}) copy-start(bf16[16,32,1024]{2,1,0:T(8,128)(2,1)S(1)} %all-to-all-done.1) | copy-start | bytes 3145732
  130.6 102.8 %reduce-scatter.13.cloned.1.call-start = ((), (), s32[]{:S(2)}) async-start(), calls=%async_computation.18 | async-start | bytes 2228224 | tf_op jit(solution)/shard_map/reduce_scatter | solution.py:84
  153.7 0.8 copy-start
  156.6 1.2 copy-start.19
  156.6 11.8 %copy-start.14 = (bf16[1,512,1024]{2,1,0:T(8,128)(2,1)S(1)}, bf16[1,512,1024]{2,1,0:T(8,128)(2,1)}, u32[]{:S(2)}) copy-start(bf16[1,512,1024]{2,1,0:T(8,128)(2,1)} %param.16) | copy-start | bytes 3145732
  156.6 11.8 %copy-start.17 = (bf16[1,512,256]{2,1,0:T(8,128)(2,1)S(1)}, bf16[1,512,256]{2,1,0:T(8,128)(2,1)}, u32[]{:S(2)}) copy-start(bf16[1,512,256]{2,1,0:T(8,128)(2,1)} %param.17) | copy-start | bytes 786436
  156.6 155.4 %reduce-scatter.11.cloned.1.call-start = ((), (), s32[]{:S(2)}) async-start(), calls=%async_computation.17 | async-start | bytes 3620864 | tf_op jit(solution)/shard_map/reduce_scatter | solution.py:84
  168.2 184.6 %copy-start.6 = (bf16[4,128,512]{2,1,0:T(8,128)(2,1)}, bf16[4,128,512]{2,1,0:T(8,128)(2,1)S(1)}, u32[]{:S(2)}) copy-start(bf16[4,128,512]{2,1,0:T(8,128)(2,1)S(1)} %all_to_all.46) | copy-start | bytes 1572868
  171.5 142.5 %copy-start.33 = (pred[32,32]{0,1:T(8,128)(4,1)S(1)}, pred[32,32]{0,1:T(8,128)(4,1)}, u32[]{:S(2)}) copy-start(pred[32,32]{0,1:T(8,128)(4,1)} %copy-done.32) | copy-start | bytes 3076
  312.0 3.6 copy-start.15
  314.2 1.8 copy-start.23
  329.5 23.3 %all-to-all-start.4 = ((bf16[16,32,1536]{2,1,0:T(8,128)(2,1)}), bf16[16,32,1536]{2,1,0:T(8,128)(2,1)S(1)}, u32[]{:S(2)}, u32[]{:S(2)}) async-start(bf16[16,32,1536]{2,1,0:T(8,128)(2,1)} %stack.31), calls=%async_computation.8 | async-start | bytes 3145728 | tf_op jit(solution)/shard_map/all_to_all | solution.py:16
  333.2 47.1 %reduce-scatter.15.cloned.1.call-start = ((), (), s32[]{:S(2)}) async-start(), calls=%async_computation.19 | async-start | bytes 1310720 | tf_op jit(solution)/shard_map/reduce_scatter | solution.py:84
  352.7 27.6 %copy-start.20 = (bf16[2,128,512]{2,1,0:T(8,128)(2,1)S(1)}, bf16[2,128,512]{2,1,0:T(8,128)(2,1)}, u32[]{:S(2)}) copy-start(bf16[2,128,512]{2,1,0:T(8,128)(2,1)} %param.11) | copy-start | bytes 786436
  356.2 112.9 %reduce-scatter.17.cloned.1.call-start = ((), (), s32[]{:S(2)}) async-start(), calls=%async_computation.20 | async-start | bytes 2228224 | tf_op jit(solution)/shard_map/reduce_scatter | solution.py:84
  380.3 11.3 %copy-start.10 = (bf16[1024,512]{1,0:T(8,128)(2,1)S(1)}, bf16[1024,512]{1,0:T(8,128)(2,1)}, u32[]{:S(2)}) copy-start(bf16[1024,512]{1,0:T(8,128)(2,1)} %copy-done.9) | copy-start | bytes 3145732
  390.8 0.8 copy-start.2
  393.7 76.4 %copy-start.22 = (f32[2,4,32,32]{2,3,1,0:T(8,128)S(1)}, f32[2,4,32,32]{2,3,1,0:T(8,128)}, u32[]{:S(2)}) copy-start(f32[2,4,32,32]{2,3,1,0:T(8,128)} %copy-done.21) | copy-start | bytes 98308
  393.7 76.4 %copy-start.26 = (bf16[32,2,128]{2,1,0:T(2,128)(2,1)S(1)}, bf16[32,2,128]{2,1,0:T(2,128)(2,1)}, u32[]{:S(2)}) copy-start(bf16[32,2,128]{2,1,0:T(2,128)(2,1)} %copy-done.25) | copy-start | bytes 49156
  393.7 76.4 %copy-start.31 = (f32[2,4,32]{2,1,0:T(4,128)S(1)}, f32[2,4,32]{2,1,0:T(4,128)}, u32[]{:S(2)}) copy-start(f32[2,4,32]{2,1,0:T(4,128)} %copy-done.30) | copy-start | bytes 3076
  393.7 77.7 %copy-start.28 = (f32[32]{0:T(128)S(1)}, f32[32]{0:T(128)}, u32[]{:S(2)}) copy-start(f32[32]{0:T(128)} %copy-done.27) | copy-start | bytes 388
  471.5 5.7 %copy-start.24 = (f32[2,4,32,32]{2,3,1,0:T(8,128)S(1)}, f32[2,4,32,32]{2,3,1,0:T(8,128)}, u32[]{:S(2)}) copy-start(f32[2,4,32,32]{2,3,1,0:T(8,128)} %copy-done.23) | copy-start | bytes 98308
  472.9 24.3 %all-to-all-start.7 = ((bf16[16,32,1536]{2,1,0:T(8,128)(2,1)}), bf16[16,32,1536]{2,1,0:T(8,128)(2,1)S(1)}, u32[]{:S(2)}, u32[]{:S(2)}) async-start(bf16[16,32,1536]{2,1,0:T(8,128)(2,1)} %stack.34), calls=%async_computation.13 | async-start | bytes 3145728 | tf_op jit(solution)/shard_map/all_to_all | solution.py:16
  498.2 20.3 %all-to-all-start.8 = ((bf16[16,32,1024]{2,1,0:T(8,128)(2,1)}), bf16[16,32,1024]{2,1,0:T(8,128)(2,1)}, u32[]{:S(2)}, u32[]{:S(2)}) async-start(bf16[16,32,1024]{2,1,0:T(8,128)(2,1)} %stack.35), calls=%async_computation.14 | async-start | bytes 2097152 | tf_op jit(solution)/shard_map/all_to_all | solution.py:16
  506.3 18.3 %copy-start.1 = (bf16[4,128,512]{2,1,0:T(8,128)(2,1)S(1)}, bf16[4,128,512]{2,1,0:T(8,128)(2,1)}, u32[]{:S(2)}) copy-start(bf16[4,128,512]{2,1,0:T(8,128)(2,1)} %copy-done) | copy-start | bytes 1572868
  506.3 18.3 %copy-start.3 = (bf16[4,128,512]{2,1,0:T(8,128)(2,1)S(1)}, bf16[4,128,512]{2,1,0:T(8,128)(2,1)}, u32[]{:S(2)}) copy-start(bf16[4,128,512]{2,1,0:T(8,128)(2,1)} %copy-done.2) | copy-start | bytes 1572868
  506.3 23.9 %collective-permute-start.3 = (bf16[512,1536]{1,0:T(8,128)(2,1)}, bf16[512,1536]{1,0:T(8,128)(2,1)S(1)}, u32[]{:S(2)}, u32[]{:S(2)}) collective-permute-start(bf16[512,1536]{1,0:T(8,128)(2,1)} %get-tuple-element.11), channel_id=1, source_target_pairs={{0,64},{64,0},{1,65},{65,1},{2,66},{66,2},{3,67},{67,3},{4,68},{68... | collective-permute-start | bytes 4718600 | tf_op jit(solution)/shard_map/ppermute | solution.py:175
  520.2 4.7 copy-start.5
  520.2 4.7 copy-start.7
  520.2 6.7 %collective-permute-start.4 = (bf16[512,1024]{1,0:T(8,128)(2,1)S(1)}, bf16[512,1024]{1,0:T(8,128)(2,1)S(1)}, u32[]{:S(2)}, u32[]{:S(2)}) collective-permute-start(bf16[512,1024]{1,0:T(8,128)(2,1)S(1)} %get-tuple-element.13), channel_id=1, source_target_pairs={{0,64},{64,0},{1,65},{65,1},{2,66},{66,2},{3,67},{67,3},{4,68},{68... | collective-permute-start | bytes 3145736 | tf_op jit(solution)/shard_map/ppermute | solution.py:175
  524.7 2.9 collective-permute-start.5
  525.0 5.2 collective-permute-start.2
  527.6 2.6 copy-start.12
Sparse Core Ops, SparseCore 0:
  30.5 73.9 reduce-scatter.6
  130.7 27.0 reduce-scatter.8
  162.0 71.3 reduce-scatter.12
  236.6 75.2 reduce-scatter.10
  356.3 23.9 reduce-scatter.14
  393.9 75.2 reduce-scatter.16
